TPU v7x, 32 devices: a whole 2x2x4 slice. The times are simulated.
32 devices in a mesh: groups: 2 (over x), elec: 16 (over z, y, core).
Axes of the slice: x: 2, y: 2, z: 4, core: 2. Of those that a mesh axis runs over, the one named last changes fastest.
Arguments:
- features: bfloat16 [131072, 256], P(('groups', 'elec')), parts along dimension 0, may hold values from -6 to 6
- assignment: int32 [131072], P(('groups', 'elec')), parts along dimension 0, may hold values from 0 to 65535, as said below
- pairs: int32 [2048, 3], P(('groups', 'elec')), parts along dimension 0, may hold values from 0 to 1023, as said below
- w_query: bfloat16 [256, 256], replicated
- w_key: bfloat16 [256, 256], replicated
- w_value: bfloat16 [256, 256], replicated, may hold values from -0.375 to 0.375
- w_out: bfloat16 [256, 256], replicated, may hold values from -0.375 to 0.375
- w_mix: bfloat16 [256, 256], replicated, may hold values from -0.375 to 0.375
Outputs:
- mixed: bfloat16 [131072, 256], P(('groups', 'elec')), parts along dimension 0
There are 2 independent parts, one for each index of `groups`. A program takes and returns all parts, laid end to end along the dimension named above; an argument that names none is the same for every part. Nothing has to cross between parts.
Inputs may be any that keep to these rules, and one draw needn't show every extreme that they name: assignment is a permutation of the rows; each group of 512 rows of one walker on one device is filled from electrons of that same group. pairs[b, :] name blocks of block b's own walker (its blocks lie on the 8 devices whose index has the same remainder modulo 1024 // 512 as block b's device, 8 on each). Over the 64 reader blocks of one device, at most 25 of the listed key blocks lie on any one device (blocks d * 64 to (d + 1) * 64 - 1 lie on device d), and exactly 25 on some device.
All inputs are finite; a program needn't handle non-finite values.
Results may differ from a plain program's by a relative error of at most 0.0078.
Values may be sent and summed in bfloat16 or wider, within the bound.
A program may use at most 128 MiB of HBM per device.

v0:
```python
import jax
import jax.numpy as jnp
from jax import lax
from jax.sharding import PartitionSpec as P

HEADS = 16
SPAN = 8


def shifted(x, axis, by):
    peers = lax.axis_size(axis)
    return lax.ppermute(x, axis, [(i, (i + by) % peers) for i in range(peers)])


def layer_norm(rows):
    mean = jnp.mean(rows, axis=-1, keepdims=True)
    centred = rows - mean
    variance = jnp.mean(centred * centred, axis=-1, keepdims=True)
    return centred * lax.rsqrt(variance + 1e-05)


def slot_table(listed, block_count, capacity, position, stride):
    flattened = listed.reshape(-1)
    owner_device = flattened // block_count
    within = flattened % block_count
    entries = flattened.shape[0]
    offset = (position - owner_device // stride) % SPAN
    alike = offset[:, None] == offset[None, :]
    earlier = jnp.arange(entries)[None, :] < jnp.arange(entries)[:, None]
    ranking = jnp.sum(jnp.where(alike & earlier, 1, 0), axis=1).astype(jnp.int32)
    slots = offset * capacity + ranking
    matches = slots[None, :] == jnp.arange(SPAN * capacity, dtype=jnp.int32)[:, None]
    tables = jnp.sum(jnp.where(matches, within[None, :], 0), axis=1)
    return (slots, tables.reshape(SPAN, capacity))


def body(features, assignment, pairs, w_query, w_key, w_value, w_out, w_mix):
    rows_dev, width = features.shape
    block_count, pair_count = pairs.shape
    cluster = rows_dev // block_count
    heads = HEADS
    head_width = width // heads
    capacity = (block_count * pair_count + SPAN - 1) // SPAN + 1
    stride = lax.axis_size("elec") // SPAN
    device_index = lax.axis_index("elec")
    position = device_index // stride
    local_rows = assignment - device_index * rows_dev
    placed = jnp.take(features, local_rows, axis=0)
    normed = layer_norm(placed.astype(jnp.float32)).astype(jnp.bfloat16)
    query = jnp.dot(normed, w_query, preferred_element_type=jnp.float32).astype(jnp.bfloat16)
    w_both = jnp.concatenate([w_key, w_value], axis=1)
    own_pairs = jnp.dot(normed, w_both, preferred_element_type=jnp.float32).astype(jnp.bfloat16)
    own_blocks = own_pairs.reshape(block_count, cluster, 2 * width)
    slots, tables = slot_table(pairs, block_count, capacity, position, stride)
    wanted_rows = [tables[0]]
    for offset_step in range(1, SPAN):
        incoming = shifted(tables[offset_step], "elec", -offset_step * stride)
        wanted_rows.append(incoming)
    demanded = jnp.stack(wanted_rows)
    outgoing = [jnp.take(own_blocks, demanded[step], axis=0) for step in range(SPAN)]
    pieces = [outgoing[0]]
    for offset_step in range(1, SPAN):
        pieces.append(shifted(outgoing[offset_step], "elec", offset_step * stride))
    arrived = jnp.stack(pieces).reshape(SPAN * capacity, cluster, 2 * width)
    remote = jnp.take(arrived, slots, axis=0).reshape(block_count, pair_count, cluster, 2 * width)
    query_blocks = query.reshape(block_count, cluster, width)
    scale = 1.0 / head_width**0.5

    def attend(args):
        block_query, own_block, listed = args
        gathered = jnp.concatenate([own_block[None], listed], axis=0).reshape(-1, 2 * width)
        set_keys = gathered[:, :width].reshape(-1, heads, head_width)
        set_values = gathered[:, width:].reshape(-1, heads, head_width)
        heads_query = block_query.reshape(cluster, heads, head_width)
        scores = (
            jnp.einsum("qhd,khd->hqk", heads_query, set_keys, preferred_element_type=jnp.float32)
            * scale
        )
        weights = jax.nn.softmax(scores, axis=-1).astype(jnp.bfloat16)
        result = jnp.einsum("hqk,khd->qhd", weights, set_values, preferred_element_type=jnp.float32)
        return result.astype(jnp.bfloat16).reshape(cluster, width)

    attended = lax.map(attend, (query_blocks, own_blocks, remote), batch_size=8)
    attended = attended.reshape(rows_dev, width)
    middle = (
        placed.astype(jnp.float32) + jnp.dot(attended, w_out, preferred_element_type=jnp.float32)
    ).astype(jnp.bfloat16)
    second = layer_norm(middle.astype(jnp.float32)).astype(jnp.bfloat16)
    mixed = middle.astype(jnp.float32) + jnp.tanh(
        jnp.dot(second, w_mix, preferred_element_type=jnp.float32)
    )
    return mixed.astype(jnp.bfloat16)


def solution(mesh):
    placed = (
        P(("groups", "elec"), None),
        P(("groups", "elec")),
        P(("groups", "elec"), None),
        P(),
        P(),
        P(),
        P(),
        P(),
    )
    return jax.shard_map(
        body, mesh=mesh, in_specs=placed, out_specs=P(("groups", "elec"), None), check_vma=False
    )
```

profile of v0, /device:TPU:13, one launch (start us, length us, event | category | flops | bytes accessed | tf_op | source)
XLA Modules:
  0.0 499.8 jit_solution(3416347615789687061)
XLA Ops:
  1.7 4.3 collective-permute-start.4
  10.0 17.0 %gather_fusion = bf16[4096,256]{1,0:T(8,128)(2,1)} fusion(bf16[4096,256]{1,0:T(8,128)(2,1)S(1)} %copy-done, s32[4096]{0:T(1024)S(1)} %fusion.40), kind=kCustom, calls=%fused_computation.8 | custom fusion | bytes 4210688 | tf_op jit(solution)/shard_map/jit(_take)/gather | solution.py:48
  33.7 3.3 convolution_convert_fusion
  47.0 4.1 gather_fusion.4
  55.0 4.1 gather_fusion.5
  59.1 4.1 gather_fusion.6
  63.2 4.1 gather_fusion.7
  78.4 4.1 gather_fusion.8
  89.7 27.3 %collective-permute-done.3 = bf16[25,64,512]{2,1,0:T(8,128)(2,1)} collective-permute-done((bf16[25,64,512]{2,1,0:T(8,128)(2,1)}, bf16[25,64,512]{2,1,0:T(8,128)(2,1)}, u32[]{:S(2)}, u32[]{:S(2)}) %collective-permute-start.3) | collective-permute-done | bytes 1638432 | tf_op jit(solution)/shard_map/ppermute | solution.py:12
  122.6 168.1 %collective-permute-done.5 = bf16[25,64,512]{2,1,0:T(8,128)(2,1)} collective-permute-done((bf16[25,64,512]{2,1,0:T(8,128)(2,1)}, bf16[25,64,512]{2,1,0:T(8,128)(2,1)}, u32[]{:S(2)}, u32[]{:S(2)}) %collective-permute-start.5) | collective-permute-done | bytes 1638432 | tf_op jit(solution)/shard_map/ppermute | solution.py:12
  293.4 32.4 %collective-permute-done.7 = bf16[25,64,512]{2,1,0:T(8,128)(2,1)} collective-permute-done((bf16[25,64,512]{2,1,0:T(8,128)(2,1)}, bf16[25,64,512]{2,1,0:T(8,128)(2,1)}, u32[]{:S(2)}, u32[]{:S(2)}) %collective-permute-start.7) | collective-permute-done | bytes 1638432 | tf_op jit(solution)/shard_map/ppermute | solution.py:12
  332.7 6.9 %collective-permute-done.13 = bf16[25,64,512]{2,1,0:T(8,128)(2,1)S(1)} collective-permute-done((bf16[25,64,512]{2,1,0:T(8,128)(2,1)S(1)}, bf16[25,64,512]{2,1,0:T(8,128)(2,1)S(1)}, u32[]{:S(2)}, u32[]{:S(2)}) %collective-permute-start.13) | collective-permute-done | bytes 1638432 | tf_op jit(solution)/shard_map/ppermute | solution.py:12
  340.9 12.9 %gather_fusion.1 = bf16[192,64,512]{2,1,0:T(8,128)(2,1)} fusion(bf16[200,64,512]{2,1,0:T(8,128)(2,1)} %bitcast.100, s32[1024]{0:T(1024)S(1)} %pad_clamp_fusion), kind=kCustom, calls=%fused_computation.9 | custom fusion | bytes 25166592 | tf_op jit(solution)/shard_map/jit(_take)/gather | solution.py:65
  353.8 10.7 %broadcast_select_fusion = bf16[8,8,3,64,512]{4,3,2,1,0:T(8,128)(2,1)} fusion(bf16[8,8,3,64,512]{4,3,2,1,0:T(8,128)(2,1)} %bitcast.98, pred[8,8,3]{2,1,0:T(8,128)(4,1)S(1)} %compare_and_fusion), kind=kLoop, calls=%fused_computation.25 | loop fusion | flops 6291456 | bytes 25166016 | tf_op jit(solution)/shard_map/jit(_take)/select_n | solution.py:65
  364.5 124.7 %while.10 = (s32[]{:T(128)}, bf16[8,8,64,256]{3,2,1,0:T(8,128)(2,1)}, bf16[8,8,64,512]{3,2,1,0:T(8,128)(2,1)}, bf16[8,8,3,64,512]{4,3,2,1,0:T(8,128)(2,1)}, bf16[8,8,64,256]{3,2,1,0:T(8,128)(2,1)}, /*index=5*/s32[]{:T(128)}) while((s32[]{:T(128)}, bf16[8,8,64,256]{3,2,1,0:T(8,128)(2,1)}, bf16[8,8,64,512]{3,2,1,0:T(8,128)(2,1)}, ...), condition=%wide.region_7.9_spmd, body=%wide.region_4.8_spmd.sunk | while | flops 145883392 | bytes 38339152 | solution.py:83
  369.4 5.1 %fusion.70 = (f32[8,16,64]{2,1,0:T(8,128)S(1)}, f32[8,16,64,256]{3,2,1,0:T(8,128)}) fusion(bf16[8,64,16,16]{1,3,2,0:T(8,128)(2,1)S(1)} %bitcast.97, bf16[8,256,16,16]{1,3,2,0:T(8,128)(2,1)S(1)} %bitcast.87), kind=kOutput, calls=%fused_computation.165.clone.1 | convolution fusion | flops 73400576 | bytes 9732096 | tf_op jit(solution)/shard_map/while/body/eval_jaxpr/vmap()/sub | solution.py:79
  375.0 4.2 fusion.71
  385.0 5.1 %fusion.70 = (f32[8,16,64]{2,1,0:T(8,128)S(1)}, f32[8,16,64,256]{3,2,1,0:T(8,128)}) fusion(bf16[8,64,16,16]{1,3,2,0:T(8,128)(2,1)S(1)} %bitcast.97, bf16[8,256,16,16]{1,3,2,0:T(8,128)(2,1)S(1)} %bitcast.87), kind=kOutput, calls=%fused_computation.165.clone.1 | convolution fusion | flops 73400576 | bytes 9732096 | tf_op jit(solution)/shard_map/while/body/eval_jaxpr/vmap()/sub | solution.py:79
  390.6 4.2 fusion.71
  400.6 5.1 %fusion.70 = (f32[8,16,64]{2,1,0:T(8,128)S(1)}, f32[8,16,64,256]{3,2,1,0:T(8,128)}) fusion(bf16[8,64,16,16]{1,3,2,0:T(8,128)(2,1)S(1)} %bitcast.97, bf16[8,256,16,16]{1,3,2,0:T(8,128)(2,1)S(1)} %bitcast.87), kind=kOutput, calls=%fused_computation.165.clone.1 | convolution fusion | flops 73400576 | bytes 9732096 | tf_op jit(solution)/shard_map/while/body/eval_jaxpr/vmap()/sub | solution.py:79
  406.2 4.2 fusion.71
  416.2 5.1 %fusion.70 = (f32[8,16,64]{2,1,0:T(8,128)S(1)}, f32[8,16,64,256]{3,2,1,0:T(8,128)}) fusion(bf16[8,64,16,16]{1,3,2,0:T(8,128)(2,1)S(1)} %bitcast.97, bf16[8,256,16,16]{1,3,2,0:T(8,128)(2,1)S(1)} %bitcast.87), kind=kOutput, calls=%fused_computation.165.clone.1 | convolution fusion | flops 73400576 | bytes 9732096 | tf_op jit(solution)/shard_map/while/body/eval_jaxpr/vmap()/sub | solution.py:79
  421.8 4.2 fusion.71
  431.8 5.1 %fusion.70 = (f32[8,16,64]{2,1,0:T(8,128)S(1)}, f32[8,16,64,256]{3,2,1,0:T(8,128)}) fusion(bf16[8,64,16,16]{1,3,2,0:T(8,128)(2,1)S(1)} %bitcast.97, bf16[8,256,16,16]{1,3,2,0:T(8,128)(2,1)S(1)} %bitcast.87), kind=kOutput, calls=%fused_computation.165.clone.1 | convolution fusion | flops 73400576 | bytes 9732096 | tf_op jit(solution)/shard_map/while/body/eval_jaxpr/vmap()/sub | solution.py:79
  437.3 4.2 fusion.71
  447.3 5.1 %fusion.70 = (f32[8,16,64]{2,1,0:T(8,128)S(1)}, f32[8,16,64,256]{3,2,1,0:T(8,128)}) fusion(bf16[8,64,16,16]{1,3,2,0:T(8,128)(2,1)S(1)} %bitcast.97, bf16[8,256,16,16]{1,3,2,0:T(8,128)(2,1)S(1)} %bitcast.87), kind=kOutput, calls=%fused_computation.165.clone.1 | convolution fusion | flops 73400576 | bytes 9732096 | tf_op jit(solution)/shard_map/while/body/eval_jaxpr/vmap()/sub | solution.py:79
  452.9 4.2 fusion.71
  462.9 5.1 %fusion.70 = (f32[8,16,64]{2,1,0:T(8,128)S(1)}, f32[8,16,64,256]{3,2,1,0:T(8,128)}) fusion(bf16[8,64,16,16]{1,3,2,0:T(8,128)(2,1)S(1)} %bitcast.97, bf16[8,256,16,16]{1,3,2,0:T(8,128)(2,1)S(1)} %bitcast.87), kind=kOutput, calls=%fused_computation.165.clone.1 | convolution fusion | flops 73400576 | bytes 9732096 | tf_op jit(solution)/shard_map/while/body/eval_jaxpr/vmap()/sub | solution.py:79
  468.5 4.2 fusion.71
  478.5 5.1 %fusion.70 = (f32[8,16,64]{2,1,0:T(8,128)S(1)}, f32[8,16,64,256]{3,2,1,0:T(8,128)}) fusion(bf16[8,64,16,16]{1,3,2,0:T(8,128)(2,1)S(1)} %bitcast.97, bf16[8,256,16,16]{1,3,2,0:T(8,128)(2,1)S(1)} %bitcast.87), kind=kOutput, calls=%fused_computation.165.clone.1 | convolution fusion | flops 73400576 | bytes 9732096 | tf_op jit(solution)/shard_map/while/body/eval_jaxpr/vmap()/sub | solution.py:79
  484.1 4.2 fusion.71
  495.8 4.1 copy.39
  (188 shorter events, 117.4 us)
Async XLA Ops:
  0.0 10.0 %copy-start = (bf16[4096,256]{1,0:T(8,128)(2,1)S(1)}, bf16[4096,256]{1,0:T(8,128)(2,1)}, u32[]{:S(2)}) copy-start(bf16[4096,256]{1,0:T(8,128)(2,1)} %param.12) | copy-start | bytes 6291460
  1.5 35.5 %collective-permute-start = (s32[25]{0:T(128)S(1)}, s32[25]{0:T(128)S(1)}, u32[]{:S(2)}, u32[]{:S(2)}) collective-permute-start(s32[25]{0:T(128)S(1)} %get-tuple-element.71), channel_id=1, source_target_pairs={{0,14},{1,15},{2,0},{3,1},{4,2},{5,3},{6,4},{7,5},{8,6},{9,7},{10,... | collective-permute-start | bytes 308 | tf_op jit(solution)/shard_map/ppermute | solution.py:12
  1.7 41.0 %collective-permute-start.2 = (s32[25]{0:T(128)S(1)}, s32[25]{0:T(128)S(1)}, u32[]{:S(2)}, u32[]{:S(2)}) collective-permute-start(s32[25]{0:T(128)S(1)} %get-tuple-element.70), channel_id=1, source_target_pairs={{0,12},{1,13},{2,14},{3,15},{4,0},{5,1},{6,2},{7,3},{8,4},{9,5},{1... | collective-permute-start | bytes 308 | tf_op jit(solution)/shard_map/ppermute | solution.py:12
  1.7 45.1 %collective-permute-start.4 = (s32[25]{0:T(128)S(1)}, s32[25]{0:T(128)S(1)}, u32[]{:S(2)}, u32[]{:S(2)}) collective-permute-start(s32[25]{0:T(128)S(1)} %get-tuple-element.69), channel_id=1, source_target_pairs={{0,10},{1,11},{2,12},{3,13},{4,14},{5,15},{6,0},{7,1},{8,2},{9,3},... | collective-permute-start | bytes 308 | tf_op jit(solution)/shard_map/ppermute | solution.py:12
  6.1 47.8 %collective-permute-start.8 = (s32[25]{0:T(128)S(1)}, s32[25]{0:T(128)S(1)}, u32[]{:S(2)}, u32[]{:S(2)}) collective-permute-start(s32[25]{0:T(128)S(1)} %get-tuple-element.67), channel_id=1, source_target_pairs={{0,6},{1,7},{2,8},{3,9},{4,10},{5,11},{6,12},{7,13},{8,14},{9,15},... | collective-permute-start | bytes 308 | tf_op jit(solution)/shard_map/ppermute | solution.py:12
  6.1 53.0 %collective-permute-start.6 = (s32[25]{0:T(128)S(1)}, s32[25]{0:T(128)S(1)}, u32[]{:S(2)}, u32[]{:S(2)}) collective-permute-start(s32[25]{0:T(128)S(1)} %get-tuple-element.68), channel_id=1, source_target_pairs={{0,8},{1,9},{2,10},{3,11},{4,12},{5,13},{6,14},{7,15},{8,0},{9,1},... | collective-permute-start | bytes 308 | tf_op jit(solution)/shard_map/ppermute | solution.py:12
  30.0 3.7 copy-start.2
  30.0 1.3 copy-start.6
  31.3 2.4 copy-start.7
  31.3 2.3 copy-start.8
  37.1 38.9 %collective-permute-start.12 = (s32[25]{0:T(128)S(1)}, s32[25]{0:T(128)S(1)}, u32[]{:S(2)}, u32[]{:S(2)}) collective-permute-start(s32[25]{0:T(128)S(1)} %get-tuple-element.65), channel_id=1, source_target_pairs={{0,2},{1,3},{2,4},{3,5},{4,6},{5,7},{6,8},{7,9},{8,10},{9,11},{10,... | collective-permute-start | bytes 308 | tf_op jit(solution)/shard_map/ppermute | solution.py:12
  42.7 33.4 %collective-permute-start.10 = (s32[25]{0:T(128)S(1)}, s32[25]{0:T(128)S(1)}, u32[]{:S(2)}, u32[]{:S(2)}) collective-permute-start(s32[25]{0:T(128)S(1)} %get-tuple-element.66), channel_id=1, source_target_pairs={{0,4},{1,5},{2,6},{3,7},{4,8},{5,9},{6,10},{7,11},{8,12},{9,13},{1... | collective-permute-start | bytes 308 | tf_op jit(solution)/shard_map/ppermute | solution.py:12
  46.9 41.5 %collective-permute-start.1 = (bf16[25,64,512]{2,1,0:T(8,128)(2,1)}, bf16[25,64,512]{2,1,0:T(8,128)(2,1)}, u32[]{:S(2)}, u32[]{:S(2)}) collective-permute-start(bf16[25,64,512]{2,1,0:T(8,128)(2,1)} %broadcast_select_fusion.8), channel_id=1, source_target_pairs={{0,2},{1,3},{2,4},{3,5},{4,6},{5,7},{6,8},{7,9},{8,10},{9,11},{10,... | collective-permute-start | bytes 4915208 | tf_op jit(solution)/shard_map/ppermute | solution.py:12
  53.9 63.1 %collective-permute-start.3 = (bf16[25,64,512]{2,1,0:T(8,128)(2,1)}, bf16[25,64,512]{2,1,0:T(8,128)(2,1)}, u32[]{:S(2)}, u32[]{:S(2)}) collective-permute-start(bf16[25,64,512]{2,1,0:T(8,128)(2,1)} %broadcast_select_fusion.7), channel_id=1, source_target_pairs={{0,4},{1,5},{2,6},{3,7},{4,8},{5,9},{6,10},{7,11},{8,12},{9,13},{1... | collective-permute-start | bytes 4915208 | tf_op jit(solution)/shard_map/ppermute | solution.py:12
  67.3 3.0 copy-start.4
  70.3 2.0 copy-start.3
  73.7 217.0 %collective-permute-start.5 = (bf16[25,64,512]{2,1,0:T(8,128)(2,1)}, bf16[25,64,512]{2,1,0:T(8,128)(2,1)}, u32[]{:S(2)}, u32[]{:S(2)}) collective-permute-start(bf16[25,64,512]{2,1,0:T(8,128)(2,1)} %broadcast_select_fusion.6), channel_id=1, source_target_pairs={{0,6},{1,7},{2,8},{3,9},{4,10},{5,11},{6,12},{7,13},{8,14},{9,15},... | collective-permute-start | bytes 4915208 | tf_op jit(solution)/shard_map/ppermute | solution.py:12
  75.9 249.8 %collective-permute-start.7 = (bf16[25,64,512]{2,1,0:T(8,128)(2,1)}, bf16[25,64,512]{2,1,0:T(8,128)(2,1)}, u32[]{:S(2)}, u32[]{:S(2)}) collective-permute-start(bf16[25,64,512]{2,1,0:T(8,128)(2,1)} %broadcast_select_fusion.5), channel_id=1, source_target_pairs={{0,8},{1,9},{2,10},{3,11},{4,12},{5,13},{6,14},{7,15},{8,0},{9,1},... | collective-permute-start | bytes 4915208 | tf_op jit(solution)/shard_map/ppermute | solution.py:12
  76.1 252.5 %collective-permute-start.9 = (bf16[25,64,512]{2,1,0:T(8,128)(2,1)}, bf16[25,64,512]{2,1,0:T(8,128)(2,1)}, u32[]{:S(2)}, u32[]{:S(2)}) collective-permute-start(bf16[25,64,512]{2,1,0:T(8,128)(2,1)} %broadcast_select_fusion.4), channel_id=1, source_target_pairs={{0,10},{1,11},{2,12},{3,13},{4,14},{5,15},{6,0},{7,1},{8,2},{9,3},... | collective-permute-start | bytes 4915208 | tf_op jit(solution)/shard_map/ppermute | solution.py:12
  82.4 1.7 copy-start.5
  88.4 242.9 %collective-permute-start.11 = (bf16[25,64,512]{2,1,0:T(8,128)(2,1)}, bf16[25,64,512]{2,1,0:T(8,128)(2,1)S(1)}, u32[]{:S(2)}, u32[]{:S(2)}) collective-permute-start(bf16[25,64,512]{2,1,0:T(8,128)(2,1)} %broadcast_select_fusion.3), channel_id=1, source_target_pairs={{0,12},{1,13},{2,14},{3,15},{4,0},{5,1},{6,2},{7,3},{8,4},{9,5},{1... | collective-permute-start | bytes 4915208 | tf_op jit(solution)/shard_map/ppermute | solution.py:12
  116.9 222.6 %collective-permute-start.13 = (bf16[25,64,512]{2,1,0:T(8,128)(2,1)S(1)}, bf16[25,64,512]{2,1,0:T(8,128)(2,1)S(1)}, u32[]{:S(2)}, u32[]{:S(2)}) collective-permute-start(bf16[25,64,512]{2,1,0:T(8,128)(2,1)S(1)} %broadcast_select_fusion.2), channel_id=1, source_target_pairs={{0,14},{1,15},{2,0},{3,1},{4,2},{5,3},{6,4},{7,5},{8,6},{9,7},{10,... | collective-permute-start | bytes 4915208 | tf_op jit(solution)/shard_map/ppermute | solution.py:12
  364.5 124.8 %copy-start.9 = (bf16[256,256]{1,0:T(8,128)(2,1)S(1)}, bf16[256,256]{1,0:T(8,128)(2,1)}, u32[]{:S(2)}) copy-start(bf16[256,256]{1,0:T(8,128)(2,1)} %param.18) | copy-start | bytes 393220
  492.3 0.9 copy-start.10
  493.2 6.6 %copy-start.1 = (bf16[4096,256]{1,0:T(8,128)(2,1)S(1)}, bf16[4096,256]{1,0:T(8,128)(2,1)}, u32[]{:S(2)}) copy-start(bf16[4096,256]{1,0:T(8,128)(2,1)} %param.12) | copy-start | bytes 6291460
where the time goes:
time: 503 us; the launch traced here: 500 us
  waiting for transfers between devices  235 us (47%)
  local copies, waits for them, and re-layouts  133 us (26%)
  matrix products  85.5 us (17%)
  other arithmetic  29.3 us (6%)
  starting transfers between devices  16.4 us (3%)
    ppermute x14, waiting for transfers between devices, shifted(): return lax.ppermute(x, axis, [(i, (i + by) % peers) for i in range(peers)])  235 us
    sub x8, matrix products, attend(): weights = jax.nn.softmax(scores, axis=-1).astype(jnp.bfloat16)  40.5 us
    dot_general x8, matrix products, attend(): jnp.einsum('hqk,khd->qhd', weights, set_values, preferred_element_type=jn...  33.7 us
    gather x8, local copies, waits for them, and re-layouts, body(): jnp.take(own_blocks, demanded[step], axis=0)  28.9 us
    gather x2, local copies, waits for them, and re-layouts, body(): placed = jnp.take(features, local_rows, axis=0)  20 us
    unnamed x29, local copies, waits for them, and re-layouts  17.1 us
    ppermute x14, starting transfers between devices, shifted(): return lax.ppermute(x, axis, [(i, (i + by) % peers) for i in range(peers)])  16.4 us
    gather x1, local copies, waits for them, and re-layouts, body(): jnp.take(arrived, slots, axis=0)  12.9 us
  transfers between devices with their start and end apart: 14, of which 4 were waited for; matrix products, arithmetic and copies ran while one was open for 17% of the time, Pallas kernels for 0%

commit v1 on v0

v1 whole, which is shorter than its diff:
```python
import functools
import math

import jax
import jax.numpy as jnp
from jax import lax
from jax.experimental import pallas as pl
from jax.experimental.pallas import tpu as pltpu
from jax.sharding import PartitionSpec as P

HEADS = 16
SPAN = 8
COPIES = 4
LANES = 128
MESH = pl.DeviceIdType.MESH


def layer_norm(rows):
    mean = jnp.mean(rows, axis=-1, keepdims=True)
    centred = rows - mean
    variance = jnp.mean(centred * centred, axis=-1, keepdims=True)
    return centred * lax.rsqrt(variance + 1e-05)


def slot_table(listed, block_count, capacity, position, stride):
    flattened = listed.reshape(-1)
    owner_device = flattened // block_count
    within = flattened % block_count
    entries = flattened.shape[0]
    offset = (position - owner_device // stride) % SPAN
    alike = offset[:, None] == offset[None, :]
    earlier = jnp.arange(entries)[None, :] < jnp.arange(entries)[:, None]
    ranking = jnp.sum(jnp.where(alike & earlier, 1, 0), axis=1).astype(jnp.int32)
    slots = offset * capacity + ranking
    columns = jnp.arange(SPAN * LANES, dtype=jnp.int32)
    matches = (offset * LANES + ranking)[None, :] == columns[:, None]
    tables = jnp.sum(jnp.where(matches, within[None, :], 0), axis=1)
    return slots, tables.astype(jnp.int32).reshape(SPAN, 1, LANES)


def place_kernel(local_ref, features_ref, placed_ref, normed_ref):
    size = features_ref.shape[0]
    one_hot = jnp.where(
        lax.broadcasted_iota(jnp.int32, (size, size), 0) == local_ref[0], 1.0, 0.0
    ).astype(jnp.bfloat16)
    placed = lax.dot_general(
        one_hot, features_ref[...], (((0,), (0,)), ((), ())), preferred_element_type=jnp.float32
    )
    placed_ref[...] = placed.astype(jnp.bfloat16)
    normed_ref[...] = layer_norm(placed).astype(jnp.bfloat16)


def exchange_kernel(
    capacity, stride, blocks_ref, tables_ref, arrived_ref,
    wanted, wanted_s, outbox, t_send, t_recv, d_send, d_recv, local_sem,
):
    me = lax.axis_index("elec")
    group = lax.axis_index("groups")
    peers = lax.axis_size("elec")
    cluster = blocks_ref.shape[1]

    def toward(step):
        return (group, lax.rem(me + step * stride + peers, peers))

    barrier = pltpu.get_barrier_semaphore()
    for step in range(1, SPAN):
        pl.semaphore_signal(barrier, inc=1, device_id=toward(step), device_id_type=MESH)
    pl.semaphore_wait(barrier, SPAN - 1)

    order = sorted(range(1, SPAN), key=lambda s: abs(s - SPAN // 2))
    asks = {}
    for step in order:
        asks[step] = pltpu.make_async_remote_copy(
            src_ref=tables_ref.at[step], dst_ref=wanted.at[step],
            send_sem=t_send.at[step], recv_sem=t_recv.at[step],
            device_id=toward(-step), device_id_type=MESH,
        )
        asks[step].start()

    def gather(step, source):
        copy = pltpu.make_async_copy(source, wanted_s.at[step], local_sem.at[step])
        copy.start()
        copy.wait()

        def one(k, carry):
            start = pl.multiple_of(k * cluster, cluster)
            outbox[step, pl.ds(start, cluster), :] = blocks_ref[wanted_s[step, 0, k]]
            return carry

        lax.fori_loop(0, capacity, one, 0)

    sends = []
    for step in order:
        asks[step].wait_recv()
        gather(step, wanted.at[step])
        send = pltpu.make_async_remote_copy(
            src_ref=outbox.at[step], dst_ref=arrived_ref.at[step],
            send_sem=d_send.at[step], recv_sem=d_recv.at[step],
            device_id=toward(step), device_id_type=MESH,
        )
        send.start()
        sends.append(send)
    gather(0, tables_ref.at[0])
    own = pltpu.make_async_copy(outbox.at[0], arrived_ref.at[0], local_sem.at[SPAN])
    own.start()
    for step in order:
        asks[step].wait_send()
    own.wait()
    for send in sends:
        send.wait()


def attend_kernel(
    slots_ref, placed_ref, normed_ref, arrived_ref, wqt_ref, wk_ref, wvt_ref, wo_ref, wm_ref,
    out_ref, projected,
):
    cluster, width = arrived_ref.shape[1:]
    rows = placed_ref.shape[0]
    blocks = rows // cluster
    pair_count = slots_ref.shape[0] // (blocks * pl.num_programs(0))
    head_width = width // HEADS
    wide = COPIES * cluster
    part = COPIES * head_width
    first = pl.program_id(0) * blocks
    f32, bf16 = jnp.float32, jnp.bfloat16
    row = lax.broadcasted_iota(jnp.int32, (width, wide), 0)
    column = lax.broadcasted_iota(jnp.int32, (width, wide), 1)
    same = (row // head_width) % COPIES == column // cluster
    scale = math.log2(math.e) / head_width**0.5
    keep = jnp.where(same, scale, 0.0).astype(f32)
    nt = (((1,), (1,)), ((), ()))

    def one(j, carry):
        start = pl.multiple_of(j * cluster, cluster)
        own = normed_ref[pl.ds(start, cluster), :]
        base = (first + j) * pair_count
        listed = [arrived_ref[slots_ref[base + p]] for p in range(pair_count)]
        key_rows = jnp.concatenate([own] + listed, axis=0)
        query = lax.dot_general(
            wqt_ref[...], jnp.concatenate([own] * COPIES, axis=0), nt, preferred_element_type=f32
        )
        query = (query * keep).astype(bf16)
        keys = jnp.dot(key_rows, wk_ref[...], preferred_element_type=f32).astype(bf16)
        values = lax.dot_general(wvt_ref[...], key_rows, nt, preferred_element_type=f32).astype(bf16)
        pieces = []
        blank = jnp.zeros((part, wide), bf16)
        for g in range(HEADS // COPIES):
            band = g * part // LANES * LANES
            mine = query[g * part : (g + 1) * part, :]
            halves = [blank] * (LANES // part)
            halves[(g * part - band) // part] = mine
            scores = jnp.dot(
                keys[:, band : band + LANES], jnp.concatenate(halves, axis=0),
                preferred_element_type=f32,
            )
            top = jnp.max(scores, axis=0, keepdims=True)
            weights = jnp.exp2(scores - top)
            total = jnp.sum(weights, axis=0, keepdims=True)
            result = jnp.dot(
                values[g * part : (g + 1) * part, :], weights.astype(bf16),
                preferred_element_type=f32,
            )
            pieces.append(result * (1.0 / total))
        attended = jnp.where(same, jnp.concatenate(pieces, axis=0), 0.0).astype(bf16)
        spread = jnp.dot(attended.T, wo_ref[...], preferred_element_type=f32)
        total = spread[:cluster]
        for c in range(1, COPIES):
            total = total + spread[c * cluster : (c + 1) * cluster]
        projected[pl.ds(start, cluster), :] = total
        return carry

    lax.fori_loop(0, blocks, one, 0, unroll=2)
    middle = (placed_ref[...].astype(f32) + projected[...]).astype(bf16)
    middle = middle.astype(f32)
    second = layer_norm(middle).astype(bf16)
    mixed = middle + jnp.tanh(jnp.dot(second, wm_ref[...], preferred_element_type=f32))
    out_ref[...] = mixed.astype(bf16)


def body(features, assignment, pairs, w_query, w_key, w_value, w_out, w_mix):
    rows_dev, width = features.shape
    block_count, pair_count = pairs.shape
    cluster = rows_dev // block_count
    capacity = (block_count * pair_count + SPAN - 1) // SPAN + 1
    stride = lax.axis_size("elec") // SPAN
    device_index = lax.axis_index("elec")
    position = device_index // stride
    group_rows = SPAN * cluster
    groups = rows_dev // group_rows
    bf16 = jnp.bfloat16

    local = (assignment - device_index * rows_dev).reshape(groups, 1, group_rows)
    local = local - group_rows * jnp.arange(groups, dtype=jnp.int32)[:, None, None]
    tile = pl.BlockSpec((group_rows, width), lambda i: (i, 0))
    placed, normed = pl.pallas_call(
        place_kernel,
        grid=(groups,),
        in_specs=[pl.BlockSpec((1, 1, group_rows), lambda i: (i, 0, 0)), tile],
        out_specs=[tile, tile],
        out_shape=[jax.ShapeDtypeStruct((rows_dev, width), bf16)] * 2,
    )(local, features)

    slots, tables = slot_table(pairs, block_count, capacity, position, stride)
    arrived = pl.pallas_call(
        functools.partial(exchange_kernel, capacity, stride),
        in_specs=[pl.BlockSpec(memory_space=pltpu.VMEM)] * 2,
        out_specs=pl.BlockSpec(memory_space=pl.ANY),
        out_shape=jax.ShapeDtypeStruct((SPAN, capacity * cluster, width), bf16),
        scratch_shapes=[
            pltpu.VMEM((SPAN, 1, LANES), jnp.int32),
            pltpu.SMEM((SPAN, 1, LANES), jnp.int32),
            pltpu.VMEM((SPAN, capacity * cluster, width), bf16),
            pltpu.SemaphoreType.DMA((SPAN,)),
            pltpu.SemaphoreType.DMA((SPAN,)),
            pltpu.SemaphoreType.DMA((SPAN,)),
            pltpu.SemaphoreType.DMA((SPAN,)),
            pltpu.SemaphoreType.DMA((SPAN + 1,)),
        ],
        compiler_params=pltpu.CompilerParams(
            collective_id=0, has_side_effects=True, vmem_limit_bytes=32 * 2**20
        ),
    )(normed.reshape(block_count, cluster, width), tables)
    arrived = arrived.reshape(SPAN * capacity, cluster, width)

    tile = pl.BlockSpec((group_rows, width), lambda i, s: (i, 0))
    weight = pl.BlockSpec((width, width), lambda i, s: (0, 0))
    return pl.pallas_call(
        attend_kernel,
        grid_spec=pltpu.PrefetchScalarGridSpec(
            num_scalar_prefetch=1,
            grid=(groups,),
            in_specs=[
                tile,
                tile,
                pl.BlockSpec(arrived.shape, lambda i, s: (0, 0, 0)),
            ]
            + [weight] * 5,
            out_specs=tile,
            scratch_shapes=[pltpu.VMEM((group_rows, width), jnp.float32)],
        ),
        out_shape=jax.ShapeDtypeStruct((rows_dev, width), bf16),
        compiler_params=pltpu.CompilerParams(vmem_limit_bytes=48 * 2**20),
    )(slots, placed, normed, arrived, w_query.T, w_key, w_value.T, w_out, w_mix)


def solution(mesh):
    placed = (
        P(("groups", "elec"), None),
        P(("groups", "elec")),
        P(("groups", "elec"), None),
        P(),
        P(),
        P(),
        P(),
        P(),
    )
    return jax.shard_map(
        body, mesh=mesh, in_specs=placed, out_specs=P(("groups", "elec"), None), check_vma=False
    )
```

time: 503 us -> 270 us (0.54)
  Pallas kernels: 0 us -> 261 us
  waiting for transfers between devices: 235 us -> 0 us
  local copies, waits for them, and re-layouts: 133 us -> 7.26 us
  matrix products: 85.5 us -> 0 us
  other arithmetic: 29.3 us -> 1.78 us
  starting transfers between devices: 16.4 us -> 0 us
    pallas_call x0 -> x3, Pallas kernels: none -> 261 us  [the longest x1 149 us: body(): pl.pallas_call(functools.partial(exchange_kernel, capacity, stride), in_s...]
    ppermute x14 -> x0, waiting for transfers between devices: 235 us -> none  [shifted(): return lax.ppermute(x, axis, [(i, (i + by) % peers) for i in range(peers)])]
    gather x11 -> x0, local copies, waits for them, and re-layouts: 61.8 us -> none  [the longest x8 28.9 us: body(): jnp.take(own_blocks, demanded[step], axis=0)]
    dot_general x12 -> x0, matrix products: 45 us -> none  [the longest x8 33.7 us: attend(): jnp.einsum('hqk,khd->qhd', weights, set_values, preferred_element_type=jn...]
    sub x8 -> x0, matrix products: 40.5 us -> none  [attend(): weights = jax.nn.softmax(scores, axis=-1).astype(jnp.bfloat16)]
    select_n x17 -> x1, other arithmetic: 22.4 us -> 0.03 us  [slot_table(): within = flattened % block_count]
    ppermute x14 -> x0, starting transfers between devices: 16.4 us -> none  [shifted(): return lax.ppermute(x, axis, [(i, (i + by) % peers) for i in range(peers)])]
    squeeze x8 -> x0, local copies, waits for them, and re-layouts: 12.4 us -> none  [body(): attended = lax.map(attend, (query_blocks, own_blocks, remote), batch_size=8)]
  transfers between devices with their start and end apart: 14 -> 0, of which waited for: 4 -> 0; matrix products, arithmetic and copies ran while one was open for 17% -> 0% of each run, Pallas kernels for 0% -> 0%
where the time goes in v1:
time: 270 us
  Pallas kernels  261 us (97%)
  local copies, waits for them, and re-layouts  7.26 us (3%)
    pallas_call x1, Pallas kernels, body(): pl.pallas_call(functools.partial(exchange_kernel, capacity, stride), in_s...  149 us
    pallas_call x1, Pallas kernels, body(): pl.pallas_call(attend_kernel, grid_spec=pltpu.PrefetchScalarGridSpec(num_...  104 us
    pallas_call x1, Pallas kernels, body(): pl.pallas_call(place_kernel, grid=(groups,), in_specs=[pl.BlockSpec((1, 1...  7.62 us
    unnamed x17, local copies, waits for them, and re-layouts  7.13 us

profile of v1, /device:TPU:13, one launch (start us, length us, event | category | flops | bytes accessed | tf_op | source)
XLA Modules:
  0.0 270.0 jit_solution(823663812107893367)
XLA Ops:
  0.0 0.7 broadcast_subtract_fusion.1
  0.7 0.7 broadcast_subtract_fusion.local_ref
  1.4 0.8 copy.14
  2.2 0.1 reshape.197
  2.3 0.2 select_reduce_fusion.1
  2.5 0.2 select_reduce_fusion
  2.7 1.0 copy.15
  3.7 1.0 copy.16
  4.7 7.6 %shard_map.82 = (bf16[4096,256]{1,0:T(8,128)(2,1)}, bf16[4096,256]{1,0:T(8,128)(2,1)}) custom-call(s32[8,1,512]{2,1,0:T(1,128)} %broadcast_subtract_fusion.local_ref, bf16[4096,256]{1,0:T(8,128)(2,1)} %features_ref.1), custom_call_target="tpu_custom_call" | custom-call | tf_op jit(solution)/shard_map/pallas_call | solution.py:195
  12.3 0.0 copy-start.1
  12.3 1.6 copy-done.1
  13.9 0.0 copy-start.2
  13.9 0.0 copy-start.3
  13.9 0.0 copy-start.4
  13.9 0.0 copy-start.5
  13.9 0.0 copy-start.6
  14.0 149.3 %shard_map.83 = bf16[8,1600,256]{2,1,0:T(8,128)(2,1)S(1)} custom-call(bf16[64,64,256]{2,1,0:T(8,128)(2,1)S(1)} %bitcast.7, s32[8,1,128]{2,1,0:T(1,128)S(1)} %bitcast.10), custom_call_target="tpu_custom_call" | custom-call | tf_op jit(solution)/shard_map/pallas_call | solution.py:204
  163.3 0.0 copy-start
  163.3 2.7 %copy-done = bf16[8,1600,256]{2,1,0:T(8,128)(2,1)} copy-done((bf16[8,1600,256]{2,1,0:T(8,128)(2,1)}, bf16[8,1600,256]{2,1,0:T(8,128)(2,1)S(1)}, u32[]{:S(2)}) %copy-start) | copy-done | bytes 6553624
  166.0 0.0 copy-done.2
  166.0 0.0 copy-done.3
  166.0 0.0 copy-done.4
  166.0 0.0 copy-done.5
  166.0 0.0 copy-done.6
  166.1 104.0 %shard_map.84 = bf16[4096,256]{1,0:T(8,128)(2,1)} custom-call(s32[192]{0:T(256)S(1)} %get-tuple-element.10.slots_ref, bf16[4096,256]{1,0:T(8,128)(2,1)S(1)} %copy-done.3, bf16[4096,256]{1,0:T(8,128)(2,1)S(1)} %copy-done.2, bf16[200,64,256]{2,1,0:T(8,128)(2,1)} %bitcast.6, bf16[256,256]{1,0:T(8,128)(2,1)S(1)} %bitcast.8, bf16[256,256]{1,0:T(8,128)(2,1)S(1)} %copy-done.4, ...), custom_call_target="tpu_custom_call" | custom-call | tf_op jit(solution)/shard_map/pallas_call | solution.py:227
  (3 shorter events, 0.0 us)
Async XLA Ops:
  12.3 1.6 copy-start.1
  13.9 152.1 %copy-start.2 = (bf16[4096,256]{1,0:T(8,128)(2,1)S(1)}, bf16[4096,256]{1,0:T(8,128)(2,1)}, u32[]{:S(2)}) copy-start(bf16[4096,256]{1,0:T(8,128)(2,1)} %get-tuple-element.8.normed_ref) | copy-start | bytes 6291460
  13.9 152.1 %copy-start.3 = (bf16[4096,256]{1,0:T(8,128)(2,1)S(1)}, bf16[4096,256]{1,0:T(8,128)(2,1)}, u32[]{:S(2)}) copy-start(bf16[4096,256]{1,0:T(8,128)(2,1)} %get-tuple-element.7.placed_ref) | copy-start | bytes 6291460
  13.9 152.1 %copy-start.4 = (bf16[256,256]{1,0:T(8,128)(2,1)S(1)}, bf16[256,256]{1,0:T(8,128)(2,1)}, u32[]{:S(2)}) copy-start(bf16[256,256]{1,0:T(8,128)(2,1)} %wk_ref.1) | copy-start | bytes 393220
  13.9 152.1 %copy-start.5 = (bf16[256,256]{1,0:T(8,128)(2,1)S(1)}, bf16[256,256]{1,0:T(8,128)(2,1)}, u32[]{:S(2)}) copy-start(bf16[256,256]{1,0:T(8,128)(2,1)} %wo_ref.1) | copy-start | bytes 393220
  13.9 152.1 %copy-start.6 = (bf16[256,256]{1,0:T(8,128)(2,1)S(1)}, bf16[256,256]{1,0:T(8,128)(2,1)}, u32[]{:S(2)}) copy-start(bf16[256,256]{1,0:T(8,128)(2,1)} %wm_ref.1) | copy-start | bytes 393220
  163.3 2.7 %copy-start = (bf16[8,1600,256]{2,1,0:T(8,128)(2,1)}, bf16[8,1600,256]{2,1,0:T(8,128)(2,1)S(1)}, u32[]{:S(2)}) copy-start(bf16[8,1600,256]{2,1,0:T(8,128)(2,1)S(1)} %shard_map.83) | copy-start | bytes 19660804

commit v2 on v1

--- a/solution.py
+++ b/solution.py
@@ -10,7 +10,6 @@
 
 HEADS = 16
 SPAN = 8
-COPIES = 4
 LANES = 128
 MESH = pl.DeviceIdType.MESH
 
@@ -111,67 +110,68 @@
 
 
 def attend_kernel(
-    slots_ref, placed_ref, normed_ref, arrived_ref, wqt_ref, wk_ref, wvt_ref, wo_ref, wm_ref,
-    out_ref, projected,
+    slots_ref, placed_ref, normed_ref, arrived_ref, wq_ref, wk_ref, wv_ref, wo_ref, wm_ref,
+    out_ref, queries, attended,
 ):
     cluster, width = arrived_ref.shape[1:]
     rows = placed_ref.shape[0]
     blocks = rows // cluster
     pair_count = slots_ref.shape[0] // (blocks * pl.num_programs(0))
     head_width = width // HEADS
-    wide = COPIES * cluster
-    part = COPIES * head_width
+    half = LANES // 2
+    per = half // head_width
     first = pl.program_id(0) * blocks
     f32, bf16 = jnp.float32, jnp.bfloat16
-    row = lax.broadcasted_iota(jnp.int32, (width, wide), 0)
-    column = lax.broadcasted_iota(jnp.int32, (width, wide), 1)
-    same = (row // head_width) % COPIES == column // cluster
+    lane = lax.broadcasted_iota(jnp.int32, (cluster, LANES), 1)
+    low = lane < half
+    low_keys = lax.broadcasted_iota(jnp.int32, ((pair_count + 1) * cluster, LANES), 1) < half
+    chosen = [jnp.where(lane // head_width == c, 1.0, 0.0).astype(bf16) for c in range(2 * per)]
+    own_head = lane % half // head_width
     scale = math.log2(math.e) / head_width**0.5
-    keep = jnp.where(same, scale, 0.0).astype(f32)
-    nt = (((1,), (1,)), ((), ()))
+    queries[...] = (
+        jnp.dot(normed_ref[...], wq_ref[...], preferred_element_type=f32) * scale
+    ).astype(bf16)
 
     def one(j, carry):
         start = pl.multiple_of(j * cluster, cluster)
-        own = normed_ref[pl.ds(start, cluster), :]
         base = (first + j) * pair_count
         listed = [arrived_ref[slots_ref[base + p]] for p in range(pair_count)]
-        key_rows = jnp.concatenate([own] + listed, axis=0)
-        query = lax.dot_general(
-            wqt_ref[...], jnp.concatenate([own] * COPIES, axis=0), nt, preferred_element_type=f32
-        )
-        query = (query * keep).astype(bf16)
+        key_rows = jnp.concatenate([normed_ref[pl.ds(start, cluster), :]] + listed, axis=0)
         keys = jnp.dot(key_rows, wk_ref[...], preferred_element_type=f32).astype(bf16)
-        values = lax.dot_general(wvt_ref[...], key_rows, nt, preferred_element_type=f32).astype(bf16)
-        pieces = []
-        blank = jnp.zeros((part, wide), bf16)
-        for g in range(HEADS // COPIES):
-            band = g * part // LANES * LANES
-            mine = query[g * part : (g + 1) * part, :]
-            halves = [blank] * (LANES // part)
-            halves[(g * part - band) // part] = mine
-            scores = jnp.dot(
-                keys[:, band : band + LANES], jnp.concatenate(halves, axis=0),
-                preferred_element_type=f32,
-            )
-            top = jnp.max(scores, axis=0, keepdims=True)
-            weights = jnp.exp2(scores - top)
-            total = jnp.sum(weights, axis=0, keepdims=True)
-            result = jnp.dot(
-                values[g * part : (g + 1) * part, :], weights.astype(bf16),
-                preferred_element_type=f32,
-            )
-            pieces.append(result * (1.0 / total))
-        attended = jnp.where(same, jnp.concatenate(pieces, axis=0), 0.0).astype(bf16)
-        spread = jnp.dot(attended.T, wo_ref[...], preferred_element_type=f32)
-        total = spread[:cluster]
-        for c in range(1, COPIES):
-            total = total + spread[c * cluster : (c + 1) * cluster]
-        projected[pl.ds(start, cluster), :] = total
+        values = jnp.dot(key_rows, wv_ref[...], preferred_element_type=f32)
+        for band in range(0, width, LANES):
+            query = queries[pl.ds(start, cluster), band : band + LANES]
+            band_keys = keys[:, band : band + LANES]
+            band_values = values[:, band : band + LANES]
+            folded = []
+            for side in range(2):
+                stacked = jnp.concatenate(
+                    [query * chosen[side * per + c] for c in range(per)], axis=0
+                )
+                scores = lax.dot_general(
+                    stacked, band_keys, (((1,), (1,)), ((), ())), preferred_element_type=f32
+                )
+                weights = jnp.exp2(scores - jnp.max(scores, axis=1, keepdims=True)).astype(bf16)
+                with_ones = (
+                    jnp.where(low_keys, band_values, 1.0)
+                    if side == 0
+                    else jnp.where(low_keys, 1.0, band_values)
+                ).astype(bf16)
+                result = jnp.dot(weights, with_ones, preferred_element_type=f32)
+                kept = result[(per - 1) * cluster :]
+                for c in range(per - 1):
+                    kept = jnp.where(own_head == c, result[c * cluster : (c + 1) * cluster], kept)
+                folded.append(kept)
+            numerator = jnp.where(low, folded[0], folded[1])
+            denominator = pltpu.roll(jnp.where(low, folded[1], folded[0]), half, 1)
+            attended[pl.ds(start, cluster), band : band + LANES] = (
+                numerator / denominator
+            ).astype(bf16)
         return carry
 
-    lax.fori_loop(0, blocks, one, 0, unroll=2)
-    middle = (placed_ref[...].astype(f32) + projected[...]).astype(bf16)
-    middle = middle.astype(f32)
+    lax.fori_loop(0, blocks, one, 0, unroll=True)
+    projected = jnp.dot(attended[...], wo_ref[...], preferred_element_type=f32)
+    middle = (placed_ref[...].astype(f32) + projected).astype(bf16).astype(f32)
     second = layer_norm(middle).astype(bf16)
     mixed = middle + jnp.tanh(jnp.dot(second, wm_ref[...], preferred_element_type=f32))
     out_ref[...] = mixed.astype(bf16)
@@ -236,11 +236,11 @@
             ]
             + [weight] * 5,
             out_specs=tile,
-            scratch_shapes=[pltpu.VMEM((group_rows, width), jnp.float32)],
+            scratch_shapes=[pltpu.VMEM((group_rows, width), bf16)] * 2,
         ),
         out_shape=jax.ShapeDtypeStruct((rows_dev, width), bf16),
         compiler_params=pltpu.CompilerParams(vmem_limit_bytes=48 * 2**20),
-    )(slots, placed, normed, arrived, w_query.T, w_key, w_value.T, w_out, w_mix)
+    )(slots, placed, normed, arrived, w_query, w_key, w_value, w_out, w_mix)
 
 
 def solution(mesh):

time: 270 us -> 206 us (0.76)
  Pallas kernels: 261 us -> 199 us
    pallas_call x1, Pallas kernels: 104 us -> 41.7 us  [body(): pl.pallas_call(attend_kernel, grid_spec=pltpu.PrefetchScalarGridSpec(num_...]
    unnamed x17 -> x19, local copies, waits for them, and re-layouts: 7.13 us -> 5.12 us
where the time goes in v2:
time: 206 us
  Pallas kernels  199 us (97%)
  local copies, waits for them, and re-layouts  5.26 us (3%)
    pallas_call x1, Pallas kernels, body(): pl.pallas_call(functools.partial(exchange_kernel, capacity, stride), in_s...  149 us
    pallas_call x1, Pallas kernels, body(): pl.pallas_call(attend_kernel, grid_spec=pltpu.PrefetchScalarGridSpec(num_...  41.7 us
    pallas_call x1, Pallas kernels, body(): pl.pallas_call(place_kernel, grid=(groups,), in_specs=[pl.BlockSpec((1, 1...  7.62 us
    unnamed x19, local copies, waits for them, and re-layouts  5.12 us

profile of v2, /device:TPU:13, one launch (start us, length us, event | category | flops | bytes accessed | tf_op | source)
XLA Modules:
  0.0 205.7 jit_solution(2402948998675237694)
XLA Ops:
  0.0 0.7 broadcast_subtract_fusion.1
  0.7 0.7 broadcast_subtract_fusion.local_ref
  1.4 0.8 copy.10
  2.2 0.1 reshape.197
  2.3 0.2 select_reduce_fusion.1
  2.5 0.2 select_reduce_fusion
  2.7 7.6 %shard_map.82 = (bf16[4096,256]{1,0:T(8,128)(2,1)}, bf16[4096,256]{1,0:T(8,128)(2,1)}) custom-call(s32[8,1,512]{2,1,0:T(1,128)} %broadcast_subtract_fusion.local_ref, bf16[4096,256]{1,0:T(8,128)(2,1)} %features_ref.1), custom_call_target="tpu_custom_call" | custom-call | tf_op jit(solution)/shard_map/pallas_call | solution.py:195
  10.3 0.0 copy-start.1
  10.3 1.6 copy-done.1
  11.9 0.0 copy-start.2
  11.9 0.0 copy-start.3
  11.9 0.0 copy-start.4
  11.9 0.0 copy-start.5
  11.9 0.0 copy-start.6
  11.9 0.0 copy-start.7
  12.0 0.0 copy-start.8
  12.0 149.3 %shard_map.83 = bf16[8,1600,256]{2,1,0:T(8,128)(2,1)S(1)} custom-call(bf16[64,64,256]{2,1,0:T(8,128)(2,1)S(1)} %bitcast.5, s32[8,1,128]{2,1,0:T(1,128)S(1)} %bitcast.6), custom_call_target="tpu_custom_call" | custom-call | tf_op jit(solution)/shard_map/pallas_call | solution.py:204
  161.3 0.0 copy-start
  161.3 2.7 %copy-done = bf16[8,1600,256]{2,1,0:T(8,128)(2,1)} copy-done((bf16[8,1600,256]{2,1,0:T(8,128)(2,1)}, bf16[8,1600,256]{2,1,0:T(8,128)(2,1)S(1)}, u32[]{:S(2)}) %copy-start) | copy-done | bytes 6553624
  164.0 0.0 copy-done.2
  164.0 0.0 copy-done.3
  164.0 0.0 copy-done.4
  164.0 0.0 copy-done.5
  164.1 0.0 copy-done.6
  164.1 0.0 copy-done.7
  164.1 0.0 copy-done.8
  164.1 41.7 %shard_map.84 = bf16[4096,256]{1,0:T(8,128)(2,1)} custom-call(s32[192]{0:T(256)S(1)} %get-tuple-element.10.slots_ref, bf16[4096,256]{1,0:T(8,128)(2,1)S(1)} %copy-done.3, bf16[4096,256]{1,0:T(8,128)(2,1)S(1)} %copy-done.2, bf16[200,64,256]{2,1,0:T(8,128)(2,1)} %bitcast.4, bf16[256,256]{1,0:T(8,128)(2,1)S(1)} %copy-done.4, bf16[256,256]{1,0:T(8,128)(2,1)S(1)} %copy-done.5, ...), custom_call_target="tpu_custom_call" | custom-call | tf_op jit(solution)/shard_map/pallas_call | solution.py:227
  (3 shorter events, 0.0 us)
Async XLA Ops:
  10.3 1.6 copy-start.1
  11.9 152.1 %copy-start.2 = (bf16[4096,256]{1,0:T(8,128)(2,1)S(1)}, bf16[4096,256]{1,0:T(8,128)(2,1)}, u32[]{:S(2)}) copy-start(bf16[4096,256]{1,0:T(8,128)(2,1)} %get-tuple-element.8.normed_ref) | copy-start | bytes 6291460
  11.9 152.1 %copy-start.3 = (bf16[4096,256]{1,0:T(8,128)(2,1)S(1)}, bf16[4096,256]{1,0:T(8,128)(2,1)}, u32[]{:S(2)}) copy-start(bf16[4096,256]{1,0:T(8,128)(2,1)} %get-tuple-element.7.placed_ref) | copy-start | bytes 6291460
  11.9 152.1 %copy-start.4 = (bf16[256,256]{1,0:T(8,128)(2,1)S(1)}, bf16[256,256]{1,0:T(8,128)(2,1)}, u32[]{:S(2)}) copy-start(bf16[256,256]{1,0:T(8,128)(2,1)} %wq_ref.1) | copy-start | bytes 393220
  11.9 152.1 %copy-start.5 = (bf16[256,256]{1,0:T(8,128)(2,1)S(1)}, bf16[256,256]{1,0:T(8,128)(2,1)}, u32[]{:S(2)}) copy-start(bf16[256,256]{1,0:T(8,128)(2,1)} %wk_ref.1) | copy-start | bytes 393220
  11.9 152.1 %copy-start.6 = (bf16[256,256]{1,0:T(8,128)(2,1)S(1)}, bf16[256,256]{1,0:T(8,128)(2,1)}, u32[]{:S(2)}) copy-start(bf16[256,256]{1,0:T(8,128)(2,1)} %wv_ref.1) | copy-start | bytes 393220
  11.9 152.1 %copy-start.7 = (bf16[256,256]{1,0:T(8,128)(2,1)S(1)}, bf16[256,256]{1,0:T(8,128)(2,1)}, u32[]{:S(2)}) copy-start(bf16[256,256]{1,0:T(8,128)(2,1)} %wo_ref.1) | copy-start | bytes 393220
  12.0 152.1 %copy-start.8 = (bf16[256,256]{1,0:T(8,128)(2,1)S(1)}, bf16[256,256]{1,0:T(8,128)(2,1)}, u32[]{:S(2)}) copy-start(bf16[256,256]{1,0:T(8,128)(2,1)} %wm_ref.1) | copy-start | bytes 393220
  161.3 2.7 %copy-start = (bf16[8,1600,256]{2,1,0:T(8,128)(2,1)}, bf16[8,1600,256]{2,1,0:T(8,128)(2,1)S(1)}, u32[]{:S(2)}) copy-start(bf16[8,1600,256]{2,1,0:T(8,128)(2,1)S(1)} %shard_map.83) | copy-start | bytes 19660804

commit v3 on v2

--- a/solution.py
+++ b/solution.py
@@ -38,15 +38,17 @@
 
 
 def place_kernel(local_ref, features_ref, placed_ref, normed_ref):
-    size = features_ref.shape[0]
-    one_hot = jnp.where(
-        lax.broadcasted_iota(jnp.int32, (size, size), 0) == local_ref[0], 1.0, 0.0
-    ).astype(jnp.bfloat16)
-    placed = lax.dot_general(
-        one_hot, features_ref[...], (((0,), (0,)), ((), ())), preferred_element_type=jnp.float32
-    )
-    placed_ref[...] = placed.astype(jnp.bfloat16)
-    normed_ref[...] = layer_norm(placed).astype(jnp.bfloat16)
+    groups, _, size = local_ref.shape
+    lane = lax.broadcasted_iota(jnp.int32, (size, LANES), 1).astype(jnp.float32)
+    for i in range(groups):
+        rows = pl.ds(i * size, size)
+        takes = jnp.broadcast_to(local_ref[i].astype(jnp.float32), (LANES, size)).T
+        one_hot = jnp.concatenate(
+            [jnp.where(takes == lane + k, 1.0, 0.0) for k in range(0, size, LANES)], axis=1
+        ).astype(jnp.bfloat16)
+        placed = jnp.dot(one_hot, features_ref[rows, :], preferred_element_type=jnp.float32)
+        placed_ref[rows, :] = placed.astype(jnp.bfloat16)
+        normed_ref[rows, :] = layer_norm(placed).astype(jnp.bfloat16)
 
 
 def exchange_kernel(
@@ -191,11 +193,12 @@
 
     local = (assignment - device_index * rows_dev).reshape(groups, 1, group_rows)
     local = local - group_rows * jnp.arange(groups, dtype=jnp.int32)[:, None, None]
-    tile = pl.BlockSpec((group_rows, width), lambda i: (i, 0))
+    batch = math.gcd(groups, 2)
+    tile = pl.BlockSpec((batch * group_rows, width), lambda i: (i, 0))
     placed, normed = pl.pallas_call(
         place_kernel,
-        grid=(groups,),
-        in_specs=[pl.BlockSpec((1, 1, group_rows), lambda i: (i, 0, 0)), tile],
+        grid=(groups // batch,),
+        in_specs=[pl.BlockSpec((batch, 1, group_rows), lambda i: (i, 0, 0)), tile],
         out_specs=[tile, tile],
         out_shape=[jax.ShapeDtypeStruct((rows_dev, width), bf16)] * 2,
     )(local, features)

time: 206 us -> 204 us (level)
  Pallas kernels: 199 us -> 196 us
    pallas_call x1, Pallas kernels: 7.62 us -> 5.38 us  [body(): pl.pallas_call(place_kernel, grid=(groups // batch,), in_specs=[pl.BlockS...]
where the time goes in v3:
time: 204 us; the launch traced here: 203 us
  Pallas kernels  196 us (96%)
  local copies, waits for them, and re-layouts  5.26 us (3%)
    pallas_call x1, Pallas kernels, body(): pl.pallas_call(functools.partial(exchange_kernel, capacity, stride), in_s...  149 us
    pallas_call x1, Pallas kernels, body(): pl.pallas_call(attend_kernel, grid_spec=pltpu.PrefetchScalarGridSpec(num_...  41.7 us
    pallas_call x1, Pallas kernels, body(): pl.pallas_call(place_kernel, grid=(groups // batch,), in_specs=[pl.BlockS...  5.38 us
    unnamed x19, local copies, waits for them, and re-layouts  5.12 us

profile of v3, /device:TPU:13, one launch (start us, length us, event | category | flops | bytes accessed | tf_op | source)
XLA Modules:
  0.0 203.5 jit_solution(15862189000675266589)
XLA Ops:
  0.0 0.7 broadcast_subtract_fusion.1
  0.7 0.7 broadcast_subtract_fusion.local_ref
  1.4 0.8 copy.10
  2.2 0.1 reshape.197
  2.3 0.2 select_reduce_fusion.1
  2.5 0.2 select_reduce_fusion
  2.7 5.4 %shard_map.82 = (bf16[4096,256]{1,0:T(8,128)(2,1)}, bf16[4096,256]{1,0:T(8,128)(2,1)}) custom-call(s32[8,1,512]{2,1,0:T(1,128)} %broadcast_subtract_fusion.local_ref, bf16[4096,256]{1,0:T(8,128)(2,1)} %features_ref.1), custom_call_target="tpu_custom_call" | custom-call | tf_op jit(solution)/shard_map/pallas_call | solution.py:198
  8.1 0.0 copy-start.1
  8.1 1.6 copy-done.1
  9.7 0.0 copy-start.2
  9.7 0.0 copy-start.3
  9.7 0.0 copy-start.4
  9.7 0.0 copy-start.5
  9.7 0.0 copy-start.6
  9.7 0.0 copy-start.7
  9.7 0.0 copy-start.8
  9.7 149.3 %shard_map.83 = bf16[8,1600,256]{2,1,0:T(8,128)(2,1)S(1)} custom-call(bf16[64,64,256]{2,1,0:T(8,128)(2,1)S(1)} %bitcast.5, s32[8,1,128]{2,1,0:T(1,128)S(1)} %bitcast.6), custom_call_target="tpu_custom_call" | custom-call | tf_op jit(solution)/shard_map/pallas_call | solution.py:207
  159.0 0.0 copy-start
  159.1 2.7 %copy-done = bf16[8,1600,256]{2,1,0:T(8,128)(2,1)} copy-done((bf16[8,1600,256]{2,1,0:T(8,128)(2,1)}, bf16[8,1600,256]{2,1,0:T(8,128)(2,1)S(1)}, u32[]{:S(2)}) %copy-start) | copy-done | bytes 6553624
  161.8 0.0 copy-done.2
  161.8 0.0 copy-done.3
  161.8 0.0 copy-done.4
  161.8 0.0 copy-done.5
  161.8 0.0 copy-done.6
  161.8 0.0 copy-done.7
  161.8 0.0 copy-done.8
  161.8 41.7 %shard_map.84 = bf16[4096,256]{1,0:T(8,128)(2,1)} custom-call(s32[192]{0:T(256)S(1)} %get-tuple-element.10.slots_ref, bf16[4096,256]{1,0:T(8,128)(2,1)S(1)} %copy-done.3, bf16[4096,256]{1,0:T(8,128)(2,1)S(1)} %copy-done.2, bf16[200,64,256]{2,1,0:T(8,128)(2,1)} %bitcast.4, bf16[256,256]{1,0:T(8,128)(2,1)S(1)} %copy-done.4, bf16[256,256]{1,0:T(8,128)(2,1)S(1)} %copy-done.5, ...), custom_call_target="tpu_custom_call" | custom-call | tf_op jit(solution)/shard_map/pallas_call | solution.py:230
  (3 shorter events, 0.0 us)
Async XLA Ops:
  8.1 1.6 copy-start.1
  9.7 152.1 %copy-start.2 = (bf16[4096,256]{1,0:T(8,128)(2,1)S(1)}, bf16[4096,256]{1,0:T(8,128)(2,1)}, u32[]{:S(2)}) copy-start(bf16[4096,256]{1,0:T(8,128)(2,1)} %get-tuple-element.8.normed_ref) | copy-start | bytes 6291460
  9.7 152.1 %copy-start.3 = (bf16[4096,256]{1,0:T(8,128)(2,1)S(1)}, bf16[4096,256]{1,0:T(8,128)(2,1)}, u32[]{:S(2)}) copy-start(bf16[4096,256]{1,0:T(8,128)(2,1)} %get-tuple-element.7.placed_ref) | copy-start | bytes 6291460
  9.7 152.1 %copy-start.4 = (bf16[256,256]{1,0:T(8,128)(2,1)S(1)}, bf16[256,256]{1,0:T(8,128)(2,1)}, u32[]{:S(2)}) copy-start(bf16[256,256]{1,0:T(8,128)(2,1)} %wq_ref.1) | copy-start | bytes 393220
  9.7 152.1 %copy-start.5 = (bf16[256,256]{1,0:T(8,128)(2,1)S(1)}, bf16[256,256]{1,0:T(8,128)(2,1)}, u32[]{:S(2)}) copy-start(bf16[256,256]{1,0:T(8,128)(2,1)} %wk_ref.1) | copy-start | bytes 393220
  9.7 152.1 %copy-start.6 = (bf16[256,256]{1,0:T(8,128)(2,1)S(1)}, bf16[256,256]{1,0:T(8,128)(2,1)}, u32[]{:S(2)}) copy-start(bf16[256,256]{1,0:T(8,128)(2,1)} %wv_ref.1) | copy-start | bytes 393220
  9.7 152.1 %copy-start.7 = (bf16[256,256]{1,0:T(8,128)(2,1)S(1)}, bf16[256,256]{1,0:T(8,128)(2,1)}, u32[]{:S(2)}) copy-start(bf16[256,256]{1,0:T(8,128)(2,1)} %wo_ref.1) | copy-start | bytes 393220
  9.7 152.1 %copy-start.8 = (bf16[256,256]{1,0:T(8,128)(2,1)S(1)}, bf16[256,256]{1,0:T(8,128)(2,1)}, u32[]{:S(2)}) copy-start(bf16[256,256]{1,0:T(8,128)(2,1)} %wm_ref.1) | copy-start | bytes 393220
  159.0 2.7 %copy-start = (bf16[8,1600,256]{2,1,0:T(8,128)(2,1)}, bf16[8,1600,256]{2,1,0:T(8,128)(2,1)S(1)}, u32[]{:S(2)}) copy-start(bf16[8,1600,256]{2,1,0:T(8,128)(2,1)S(1)} %shard_map.83) | copy-start | bytes 19660804
